TPU v7x, 128 devices: a whole 4x4x4 slice. The times are simulated.
128 devices in a mesh: fsdp: 4 (over z), ctx: 32 (over x, y, core).
Axes of the slice: x: 4, y: 4, z: 4, core: 2. Of those that a mesh axis runs over, the one named last changes fastest.
Arguments:
- hidden: bfloat16 [16384, 1536], P(('fsdp', 'ctx')), may hold values from -6 to 6
- segments: int32 [16384], P(('fsdp', 'ctx')), may hold values from 0 to 3, as said below
- norm_gain: float32 [1536], replicated, may hold values from 0.5 to 8
- in_weight: bfloat16 [1536, 6448], P(('fsdp', 'ctx')), may hold values from -0.6 to 0.6
- conv_weight: float32 [4, 3328], replicated, may hold values from -3 to 3
- conv_bias: float32 [3328], replicated, may hold values from -3 to 3
- dt_bias: float32 [48], replicated, may hold values from -1 to 0.5
- a_log: float32 [48], replicated, may hold values from -14 to -2
- skip_scale: float32 [48], replicated, may hold values from 0.5 to 2
- gate_gain: float32 [3072], replicated, may hold values from 0.25 to 1.75
- out_weight: bfloat16 [1536, 3072], P(('fsdp', 'ctx')), may hold values from -0.109375 to 0.109375
- cotangent: bfloat16 [16384, 1536], P(('fsdp', 'ctx')), may hold values from -30 to 30
- in_momentum: float32 [1536, 6448], P(('fsdp', 'ctx')), may hold values from -1536 to 1536
- out_momentum: float32 [1536, 3072], P(('fsdp', 'ctx')), may hold values from -1536 to 1536
- vector_momentum: float32 [21392], replicated, may hold values from -80 to 80
Outputs:
- block_output: bfloat16 [16384, 1536], P(('fsdp', 'ctx'))
- input_grad: float32 [16384, 1536], P(('fsdp', 'ctx'))
- in_grad: float32 [1536, 6448], P(('fsdp', 'ctx'))
- in_momentum_new: float32 [1536, 6448], P(('fsdp', 'ctx'))
- in_weight_new: float32 [1536, 6448], P(('fsdp', 'ctx'))
- out_grad: float32 [1536, 3072], P(('fsdp', 'ctx'))
- out_momentum_new: float32 [1536, 3072], P(('fsdp', 'ctx'))
- out_weight_new: float32 [1536, 3072], P(('fsdp', 'ctx'))
- vector_grad: float32 [21392], replicated
- vector_momentum_new: float32 [21392], replicated
- vector_new: float32 [21392], replicated
Inputs may be any that keep to these rules, and one draw needn't show every extreme that they name: `segments`: within each sequence of 4096 positions the document numbers start at 0 and rise by one at each new document, never falling; there are 4 documents, each of 200 positions or more.
All inputs are finite; a program needn't handle non-finite values.
Results may differ from a plain program's by a relative error of at most 0.028.
Values may be sent and summed in bfloat16 or wider, within the bound.
No kernel may reach another device: no remote copies, remote signals or barrier semaphores. Data moves between devices by JAX's collectives and lax.ppermute only.
A program may use at most 320 MiB of HBM per device.

v0:
```python
import math

import jax
import jax.numpy as jnp
from jax import lax
from jax.sharding import PartitionSpec as P

GROUP = 256
NS_STEPS = 5


EPSILON = 1e-05
NORM_FLOOR = 1e-07
POLY_FIRST = 3.4445
POLY_SECOND = -4.775
POLY_THIRD = 2.0315
MATRIX_MOMENTUM = 0.95
MATRIX_RATE = 0.5
VECTOR_MOMENTUM = 0.9
VECTOR_RATE = 0.05
HIGHEST = lax.Precision.HIGHEST


def shifted(value, axis, steps):
    count = lax.axis_size(axis)
    initial, last = (max(0, -steps), min(count, count - steps))
    return lax.ppermute(value, axis, [(source, source + steps) for source in range(initial, last)])


def entering(shard, axis, join, neutral):
    place = lax.axis_index(axis)
    gathered = jax.tree.map(
        lambda a, kind: lax.all_gather(a.astype(kind), axis), shard, (jnp.bfloat16, jnp.bfloat16)
    )
    state = jax.tree.map(lambda a, e: jnp.zeros_like(a) + jnp.asarray(e, a.dtype), shard, neutral)

    def one(turn, state):
        return join(
            state,
            jax.tree.map(
                lambda a, own: lax.dynamic_index_in_dim(a, turn, 0, False).astype(own.dtype),
                gathered,
                shard,
            ),
        )

    return lax.fori_loop(0, place, one, state)


def entering_2(shard, axis, combine, identity):
    peers, here = (lax.axis_size(axis), lax.axis_index(axis))
    everything = jax.tree.map(
        lambda part, kind: lax.all_gather(part.astype(kind), axis),
        shard,
        jax.tree.map(lambda a: jnp.bfloat16 if a.dtype == jnp.float32 else a.dtype, shard),
    )
    start = jax.tree.map(
        lambda part, zero: jnp.broadcast_to(jnp.asarray(zero, part.dtype), part.shape),
        shard,
        identity,
    )

    def turn(k, before):
        at = peers - 1 - k
        reached = at > here
        new = combine(
            before, jax.tree.map(lambda part, own: part[at].astype(own.dtype), everything, shard)
        )
        return jax.tree.map(lambda a, b: jnp.where(reached, a, b), new, before)

    return lax.fori_loop(0, peers, turn, start)


def as_sent(shard):
    return jax.tree.map(lambda a: a.astype(jnp.bfloat16) if a.dtype == jnp.float32 else a, shard)


def rms_scale(values, gain_vec):
    return (
        values * lax.rsqrt(jnp.mean(values * values, axis=-1, keepdims=True) + EPSILON) * gain_vec
    )


def gate_norm(outputs, gate_in, gain_vec):
    product = outputs * jax.nn.silu(gate_in)
    return (
        product
        * lax.rsqrt(jnp.mean(product * product, axis=-1, keepdims=True) + EPSILON)
        * gain_vec
    )


def conv_section(
    conv_in,
    edge_rows,
    edge_ids,
    seg_ids,
    conv_taps,
    conv_shift,
    dt_raw,
    dt_shift,
    decay_log,
    inner_width,
    state_width,
    num_heads,
):
    row_count = conv_in.shape[0]
    taps = conv_taps.shape[0]
    extended = jnp.concatenate([edge_rows, conv_in], axis=0)
    ext_ids = jnp.concatenate([edge_ids, seg_ids], axis=0)
    conv_sum = jnp.zeros_like(conv_in) + conv_shift[None, :]
    for conv_lag in range(taps):
        offset = taps - 1 - conv_lag
        same_doc = (ext_ids[offset : offset + row_count] == seg_ids).astype(jnp.float32)
        conv_sum = (
            conv_sum
            + conv_taps[conv_lag][None, :]
            * extended[offset : offset + row_count]
            * same_doc[:, None]
        )
    active = jax.nn.silu(conv_sum)
    head_size = inner_width // num_heads
    values_in = active[:, :inner_width].reshape(row_count, num_heads, head_size)
    b_proj = active[:, inner_width : inner_width + state_width]
    c_proj = active[:, inner_width + state_width :]
    step_size = jax.nn.softplus(dt_raw + dt_shift[None, :])
    log_decay = -jnp.exp(decay_log)[None, :] * step_size
    return (values_in, b_proj, c_proj, log_decay, step_size)


def ssd_piece(chain, inputs, direct_scale):
    state_in, prev_id = chain
    values_in, b_proj, c_proj, log_decay, step_size, seg_ids = inputs
    row_count = seg_ids.shape[0]
    cumulative = jnp.cumsum(log_decay, axis=0)
    cum_heads = cumulative.T
    row_index = lax.broadcasted_iota(jnp.int32, (row_count, row_count), 0)
    col_index = lax.broadcasted_iota(jnp.int32, (row_count, row_count), 1)
    keep_mask = (row_index >= col_index) & (seg_ids[:, None] == seg_ids[None, :])
    gap_matrix = cum_heads[:, :, None] - cum_heads[:, None, :]
    decay_matrix = jnp.where(
        keep_mask[None], jnp.exp(jnp.where(keep_mask[None], gap_matrix, 0.0)), 0.0
    )
    scores = jnp.dot(c_proj, b_proj.T, precision=HIGHEST)
    mixing = decay_matrix * scores[None] * step_size.T[:, None, :]
    within = jnp.einsum("hts,shp->thp", mixing, values_in, precision=HIGHEST)
    keep_flag = (seg_ids == prev_id).astype(jnp.float32)
    carried = (
        jnp.einsum("tn,hpn->thp", c_proj, state_in, precision=HIGHEST)
        * (jnp.exp(cumulative) * keep_flag[:, None])[:, :, None]
    )
    last_cum = cumulative[-1]
    tail_weight = (
        jnp.exp(last_cum[None, :] - cumulative)
        * (seg_ids == seg_ids[-1]).astype(jnp.float32)[:, None]
        * step_size
    )
    fresh = jnp.einsum("sh,shp,sn->hpn", tail_weight, values_in, b_proj, precision=HIGHEST)
    link_gain = jnp.exp(last_cum) * (seg_ids[-1] == prev_id).astype(jnp.float32)
    new_state = link_gain[:, None, None] * state_in + fresh
    outputs = within + carried + direct_scale[None, :, None] * values_in
    return ((new_state, seg_ids[-1]), outputs)


def ssd_scan(
    values_in,
    b_proj,
    c_proj,
    log_decay,
    step_size,
    seg_ids,
    prev_id,
    state_in,
    direct_scale,
    piece_rows,
):
    row_count = seg_ids.shape[0]
    pieces = row_count // piece_rows

    def split_rows(array):
        return array.reshape((pieces, piece_rows) + array.shape[1:])

    def piece_step(chain, inputs):
        return ssd_piece(chain, inputs, direct_scale)

    stacked = (
        split_rows(values_in),
        split_rows(b_proj),
        split_rows(c_proj),
        split_rows(log_decay),
        split_rows(step_size),
        split_rows(seg_ids),
    )
    (state_out, last_id), outputs = lax.scan(
        jax.checkpoint(piece_step), (state_in, prev_id), stacked
    )
    return (outputs.reshape((row_count,) + values_in.shape[1:]), state_out)


def carry_term(log_decay, c_proj, state_in, seg_ids, prev_id):
    cumulative = jnp.cumsum(log_decay, axis=0)
    keep_flag = (seg_ids == prev_id).astype(jnp.float32)
    return (
        jnp.einsum("tn,hpn->thp", c_proj, state_in, precision=HIGHEST)
        * (jnp.exp(cumulative) * keep_flag[:, None])[:, :, None]
    )


def chain_combine(earlier, later):
    return (earlier[0] * later[0], later[0][:, None, None] * earlier[1] + later[1])


def row_product(left, right):
    return lax.dot_general(
        left, right, (((0,), (0,)), ((), ())), preferred_element_type=jnp.float32
    )


def local(
    hidden,
    segments,
    norm_gain,
    in_weight,
    conv_weight,
    conv_bias,
    dt_bias,
    a_log,
    skip_scale,
    gate_gain,
    out_weight,
    cotangent,
    in_momentum,
    out_momentum,
    vector_momentum,
):
    row_count = hidden.shape[0]
    model_width = hidden.shape[1]
    inner_width = gate_gain.shape[0]
    num_heads = skip_scale.shape[0]
    head_size = inner_width // num_heads
    proj_width = in_weight.shape[1]
    state_width = (proj_width - 2 * inner_width - num_heads) // 2
    taps = conv_weight.shape[0]
    channels = conv_weight.shape[1]
    piece_rows = min(row_count, GROUP)
    seg_ids = segments.astype(jnp.float32)
    zero_state = jnp.zeros((num_heads, head_size, state_width), jnp.float32)
    w_in_full, w_out_full = (
        lax.all_gather(in_weight, ("fsdp", "ctx"), axis=0, tiled=True),
        lax.all_gather(out_weight, ("fsdp", "ctx"), axis=0, tiled=True),
    )
    hidden_full = hidden.astype(jnp.float32)
    normed_f, norm_pull = jax.vjp(rms_scale, hidden_full, norm_gain)
    normed = normed_f.astype(jnp.bfloat16)
    projected = jnp.dot(normed, w_in_full, preferred_element_type=jnp.float32)
    gate_in = projected[:, :inner_width]
    conv_in = projected[:, inner_width : inner_width + channels]
    dt_raw = projected[:, inner_width + channels :]
    edge_rows, edge_ids = (
        shifted(conv_in[row_count - (taps - 1) :].astype(jnp.bfloat16), "ctx", 1).astype(
            jnp.float32
        ),
        shifted(seg_ids[row_count - (taps - 1) :].astype(jnp.bfloat16), "ctx", 1).astype(
            jnp.float32
        ),
    )
    prev_id = edge_ids[-1]

    def conv_local(conv_values, edge_values, conv_taps, conv_shift, dt_values, dt_shift, decay_log):
        return conv_section(
            conv_values,
            edge_values,
            edge_ids,
            seg_ids,
            conv_taps,
            conv_shift,
            dt_values,
            dt_shift,
            decay_log,
            inner_width,
            state_width,
            num_heads,
        )

    (values_in, b_proj, c_proj, log_decay, step_size), conv_pull = jax.vjp(
        conv_local, conv_in, edge_rows, conv_weight, conv_bias, dt_raw, dt_bias, a_log
    )

    def ssd_local(values_arg, b_arg, c_arg, decay_arg, step_arg, direct_arg):
        return ssd_scan(
            values_arg,
            b_arg,
            c_arg,
            decay_arg,
            step_arg,
            seg_ids,
            prev_id,
            zero_state,
            direct_arg,
            piece_rows,
        )

    (local_out, fresh), ssd_pull = jax.vjp(
        ssd_local, values_in, b_proj, c_proj, log_decay, step_size, skip_scale
    )
    link_gain = jnp.exp(jnp.sum(log_decay, axis=0)) * (seg_ids[-1] == prev_id).astype(jnp.float32)
    identity = (jnp.ones((num_heads,), jnp.float32), zero_state)
    incoming = entering((link_gain, fresh), "ctx", chain_combine, identity)[1]

    def carry_local(decay_arg, c_arg, state_arg):
        return carry_term(decay_arg, c_arg, state_arg, seg_ids, prev_id)

    carried, carry_pull = jax.vjp(carry_local, log_decay, c_proj, incoming)
    mixer_out = (local_out + carried).reshape(row_count, inner_width)
    gated_f, gate_pull = jax.vjp(gate_norm, mixer_out, gate_in, gate_gain)
    gated = gated_f.astype(jnp.bfloat16)
    mixed = lax.dot_general(
        gated, w_out_full, (((1,), (1,)), ((), ())), preferred_element_type=jnp.float32
    )
    block_output = (hidden_full + mixed).astype(jnp.bfloat16)
    w_in_back, w_out_back = (w_in_full, w_out_full)
    d_gated = jnp.dot(cotangent, w_out_back, preferred_element_type=jnp.float32)
    d_mixer, d_gate_in, d_gate_gain = gate_pull(d_gated)
    d_mixer = d_mixer.reshape(row_count, num_heads, head_size)
    d_decay_carry, d_c_carry, local_back = carry_pull(d_mixer)
    grad_state = entering_2((link_gain, local_back), "ctx", chain_combine, identity)[1]
    d_values, d_b, d_c, d_decay, d_step, d_skip = ssd_pull((d_mixer, grad_state))
    d_link = jnp.sum(grad_state * incoming, axis=(1, 2)) * link_gain
    d_decay = d_decay + d_decay_carry + d_link[None, :]
    d_c = d_c + d_c_carry
    d_conv_in, d_edge, d_conv_weight, d_conv_bias, d_dt_raw, d_dt_bias, d_a_log = conv_pull(
        (d_values, d_b, d_c, d_decay, d_step)
    )
    back_edge = shifted(as_sent(d_edge), "ctx", -1).astype(d_edge.dtype)
    d_conv_in = jnp.concatenate(
        [d_conv_in[: row_count - (taps - 1)], d_conv_in[row_count - (taps - 1) :] + back_edge],
        axis=0,
    )
    d_projected = jnp.concatenate([d_gate_in, d_conv_in, d_dt_raw], axis=1).astype(jnp.bfloat16)
    d_normed = lax.dot_general(
        d_projected, w_in_back, (((1,), (1,)), ((), ())), preferred_element_type=jnp.float32
    )
    d_hidden, d_norm_gain = norm_pull(d_normed)
    input_grad = cotangent.astype(jnp.float32) + d_hidden
    joined = lax.psum_scatter(
        jnp.concatenate([row_product(normed, d_projected), row_product(cotangent, gated)], axis=1),
        ("fsdp", "ctx"),
        scatter_dimension=0,
        tiled=True,
    )
    in_shard = joined[:, :proj_width]
    out_shard = joined[:, proj_width:]
    vector_local = jnp.concatenate(
        [
            d_norm_gain,
            d_conv_weight.reshape(-1),
            d_conv_bias,
            d_dt_bias,
            d_a_log,
            d_skip,
            d_gate_gain,
        ]
    )
    in_moment = MATRIX_MOMENTUM * in_momentum + in_shard
    out_moment = MATRIX_MOMENTUM * out_momentum + out_shard
    vector_grad, in_square, out_square = lax.psum(
        (vector_local, jnp.sum(in_moment * in_moment), jnp.sum(out_moment * out_moment)),
        ("fsdp", "ctx"),
    )
    rows_in = in_moment / (jnp.sqrt(in_square) + NORM_FLOOR)
    rows_out = out_moment / (jnp.sqrt(out_square) + NORM_FLOOR)
    for iteration in range(NS_STEPS):
        low_in = rows_in.astype(jnp.bfloat16)
        low_out = rows_out.astype(jnp.bfloat16)
        whole_in, whole_out = (
            lax.all_gather(low_in, ("fsdp", "ctx"), axis=0, tiled=True),
            lax.all_gather(low_out, ("fsdp", "ctx"), axis=0, tiled=True),
        )
        gram_in = lax.dot_general(
            low_in, whole_in, (((1,), (1,)), ((), ())), preferred_element_type=jnp.float32
        ).astype(jnp.bfloat16)
        gram_out = lax.dot_general(
            low_out, whole_out, (((1,), (1,)), ((), ())), preferred_element_type=jnp.float32
        ).astype(jnp.bfloat16)
        full_gram_in, full_gram_out = (
            lax.all_gather(gram_in, ("fsdp", "ctx"), axis=0, tiled=True),
            lax.all_gather(gram_out, ("fsdp", "ctx"), axis=0, tiled=True),
        )
        poly_in = (
            POLY_SECOND * gram_in.astype(jnp.float32)
            + POLY_THIRD * jnp.dot(gram_in, full_gram_in, preferred_element_type=jnp.float32)
        ).astype(jnp.bfloat16)
        poly_out = (
            POLY_SECOND * gram_out.astype(jnp.float32)
            + POLY_THIRD * jnp.dot(gram_out, full_gram_out, preferred_element_type=jnp.float32)
        ).astype(jnp.bfloat16)
        rows_in = POLY_FIRST * low_in.astype(jnp.float32) + jnp.dot(
            poly_in, whole_in, preferred_element_type=jnp.float32
        )
        rows_out = POLY_FIRST * low_out.astype(jnp.float32) + jnp.dot(
            poly_out, whole_out, preferred_element_type=jnp.float32
        )
    in_weight_new = (
        in_weight.astype(jnp.float32) - MATRIX_RATE * math.sqrt(proj_width / model_width) * rows_in
    )
    out_weight_new = (
        out_weight.astype(jnp.float32)
        - MATRIX_RATE * math.sqrt(inner_width / model_width) * rows_out
    )
    vector_old = jnp.concatenate(
        [norm_gain, conv_weight.reshape(-1), conv_bias, dt_bias, a_log, skip_scale, gate_gain]
    )
    vector_momentum_new = VECTOR_MOMENTUM * vector_momentum + (1.0 - VECTOR_MOMENTUM) * vector_grad
    vector_new = vector_old - VECTOR_RATE * vector_momentum_new
    return (
        block_output,
        input_grad,
        in_shard,
        in_moment,
        in_weight_new,
        out_shard,
        out_moment,
        out_weight_new,
        vector_grad,
        vector_momentum_new,
        vector_new,
    )


def solution(mesh):
    placed = (
        P(("fsdp", "ctx"), None),
        P(("fsdp", "ctx")),
        P(),
        P(("fsdp", "ctx"), None),
        P(),
        P(),
        P(),
        P(),
        P(),
        P(),
        P(("fsdp", "ctx"), None),
        P(("fsdp", "ctx"), None),
        P(("fsdp", "ctx"), None),
        P(("fsdp", "ctx"), None),
        P(),
    )
    return jax.shard_map(
        local,
        mesh=mesh,
        in_specs=placed,
        out_specs=(
            P(("fsdp", "ctx"), None),
            P(("fsdp", "ctx"), None),
            P(("fsdp", "ctx"), None),
            P(("fsdp", "ctx"), None),
            P(("fsdp", "ctx"), None),
            P(("fsdp", "ctx"), None),
            P(("fsdp", "ctx"), None),
            P(("fsdp", "ctx"), None),
            P(),
            P(),
            P(),
        ),
        check_vma=False,
    )
```

profile of v0, /device:TPU:1, one launch (start us, length us, event | category | flops | bytes accessed | tf_op | source)
XLA Modules:
  0.0 2705.6 jit_solution(273587419089277503)
XLA Ops:
  22.9 87.7 %all-gather.54.cloned.1.call-done = bf16[128,12,6448]{2,1,0:T(8,128)(2,1)} async-done(((bf16[1,12,6448]{2,1,0:T(8,128)(2,1)}), bf16[128,12,6448]{2,1,0:T(8,128)(2,1)}) %all-gather.54.cloned.1.call-update) | async-done | bytes 19808272 | tf_op jit(solution)/shard_map/all_gather | solution.py:249
  201.7 63.8 %all-reduce.12 = bf16[1536]{0:T(1024)(128)(2,1)S(1)} all-reduce(bf16[1536]{0:T(1024)(128)(2,1)S(1)} %dynamic-update-slice), channel_id=2, replica_groups=mesh['fsdp'=4,'ctx'=32] {'ctx'}, use_global_device_ids=true, to_apply=%add.12 | all-reduce | flops 1536 | bytes 6144
  332.4 114.2 %all-gather.52.cloned.1.call-done = bf16[1536,64,128]{2,1,0:T(8,128)(2,1)} async-done(((bf16[48,64,128]{2,1,0:T(8,128)(2,1)}), bf16[1536,64,128]{2,1,0:T(8,128)(2,1)}) %all-gather.52.cloned.1.call-update) | async-done | bytes 25165840 | tf_op jit(solution)/shard_map/all_gather | solution.py:53
  446.6 70.8 %while.21 = (s32[]{:T(128)}, f32[48,64,128]{2,1,0:T(8,128)S(1)}, s32[]{:T(128)}, bf16[32,48]{1,0:T(8,128)(2,1)}, bf16[32,48,64,128]{3,2,1,0:T(8,128)(2,1)}, /*index=5*/s32[]{:T(128)}, s32[]{:T(128)}, s32[]{:T(128)}, s32[]{:T(128)}) while((s32[]{:T(128)}, f32[48,64,128]{2,1,0:T(8,128)S(1)}, s32[]{:T(128)}, ...), condition=%wide.region_8.9_spmd.clone, body=%wide.region_7.8_spmd.clone.sunk | while | flops 1966136 | bytes 3932815 | solution.py:71
  608.3 39.1 %pad_maximum_fusion = f32[1536,9520]{0,1:T(8,128)} fusion(f32[1536,3072]{0,1:T(8,128)} %convolution_bitcast_fusion, f32[1536,6448]{0,1:T(8,128)} %fusion.117), kind=kLoop, calls=%fused_computation.5 | loop fusion | flops 14622720 | bytes 116981760 | tf_op jit(solution)/shard_map/concatenate | solution.py:346
  648.2 383.6 %all-reduce.18.cloned.1.call-done = (f32[1536,9520]{0,1:T(8,128)}, f32[21392]{0:T(1024)}) async-done(((f32[1536,9520]{0,1:T(8,128)}, f32[21392]{0:T(1024)}), (f32[1536,9520]{0,1:T(8,128)}, f32[21392]{0:T(1024)})) %all-reduce.18.cloned.1.call-update) | async-done | bytes 58576464
  1042.1 65.6 %all-reduce.14 = (f32[]{:T(128)}, f32[]{:T(128)}) all-reduce(f32[]{:T(128)} %get-tuple-element.468, f32[]{:T(128)} %get-tuple-element.466), channel_id=1, replica_groups=mesh['fsdp'=4,'ctx'=32] {'fsdp','ctx'}, use_global_device_ids=true, to_apply=%region_24.25 | all-reduce | flops 2 | bytes 16 | tf_op jit(solution)/shard_map/psum | solution.py:366
  1110.6 69.7 %all-gather.78.cloned.1.call-done = bf16[128,12,3072]{2,1,0:T(8,128)(2,1)} async-done(((bf16[1,12,3072]{2,1,0:T(8,128)(2,1)}), bf16[128,12,3072]{2,1,0:T(8,128)(2,1)}) %all-gather.78.cloned.1.call-update) | async-done | bytes 9437200 | tf_op jit(solution)/shard_map/all_gather | solution.py:377
  1201.0 78.4 %all-gather.58.cloned.1.call-done = bf16[128,12,6448]{2,1,0:T(8,128)(2,1)} async-done(((bf16[1,12,6448]{2,1,0:T(8,128)(2,1)}), bf16[128,12,6448]{2,1,0:T(8,128)(2,1)}) %all-gather.58.cloned.1.call-update) | async-done | bytes 19808272 | tf_op jit(solution)/shard_map/all_gather | solution.py:376
  1279.4 29.4 %reshape.448 = bf16[1536,6448]{1,0:T(8,128)(2,1)} reshape(bf16[128,12,6448]{2,1,0:T(8,128)(2,1)} %all-gather.58.cloned.1.call-done) | data formatting | bytes 39616512
  1366.8 53.5 %all-gather.60.cloned.1.call-done = bf16[128,12,1536]{2,1,0:T(8,128)(2,1)} async-done(((bf16[1,12,1536]{2,1,0:T(8,128)(2,1)}), bf16[128,12,1536]{2,1,0:T(8,128)(2,1)}) %all-gather.60.cloned.1.call-update) | async-done | bytes 4718608 | tf_op jit(solution)/shard_map/all_gather | solution.py:386
  1440.9 54.0 %all-gather.82.cloned.1.call-done = bf16[128,12,3072]{2,1,0:T(8,128)(2,1)} async-done(((bf16[1,12,3072]{2,1,0:T(8,128)(2,1)}), bf16[128,12,3072]{2,1,0:T(8,128)(2,1)}) %all-gather.82.cloned.1.call-update) | async-done | bytes 9437200 | tf_op jit(solution)/shard_map/all_gather | solution.py:377
  1515.9 78.0 %all-gather.62.cloned.1.call-done = bf16[128,12,6448]{2,1,0:T(8,128)(2,1)} async-done(((bf16[1,12,6448]{2,1,0:T(8,128)(2,1)}), bf16[128,12,6448]{2,1,0:T(8,128)(2,1)}) %all-gather.62.cloned.1.call-update) | async-done | bytes 19808272 | tf_op jit(solution)/shard_map/all_gather | solution.py:376
  1681.1 53.5 %all-gather.64.cloned.1.call-done = bf16[128,12,1536]{2,1,0:T(8,128)(2,1)} async-done(((bf16[1,12,1536]{2,1,0:T(8,128)(2,1)}), bf16[128,12,1536]{2,1,0:T(8,128)(2,1)}) %all-gather.64.cloned.1.call-update) | async-done | bytes 4718608 | tf_op jit(solution)/shard_map/all_gather | solution.py:386
  1755.2 54.0 %all-gather.86.cloned.1.call-done = bf16[128,12,3072]{2,1,0:T(8,128)(2,1)} async-done(((bf16[1,12,3072]{2,1,0:T(8,128)(2,1)}), bf16[128,12,3072]{2,1,0:T(8,128)(2,1)}) %all-gather.86.cloned.1.call-update) | async-done | bytes 9437200 | tf_op jit(solution)/shard_map/all_gather | solution.py:377
  1830.0 78.0 %all-gather.66.cloned.1.call-done = bf16[128,12,6448]{2,1,0:T(8,128)(2,1)} async-done(((bf16[1,12,6448]{2,1,0:T(8,128)(2,1)}), bf16[128,12,6448]{2,1,0:T(8,128)(2,1)}) %all-gather.66.cloned.1.call-update) | async-done | bytes 19808272 | tf_op jit(solution)/shard_map/all_gather | solution.py:376
  1995.3 53.4 %all-gather.68.cloned.1.call-done = bf16[128,12,1536]{2,1,0:T(8,128)(2,1)} async-done(((bf16[1,12,1536]{2,1,0:T(8,128)(2,1)}), bf16[128,12,1536]{2,1,0:T(8,128)(2,1)}) %all-gather.68.cloned.1.call-update) | async-done | bytes 4718608 | tf_op jit(solution)/shard_map/all_gather | solution.py:386
  2069.3 54.0 %all-gather.90.cloned.1.call-done = bf16[128,12,3072]{2,1,0:T(8,128)(2,1)} async-done(((bf16[1,12,3072]{2,1,0:T(8,128)(2,1)}), bf16[128,12,3072]{2,1,0:T(8,128)(2,1)}) %all-gather.90.cloned.1.call-update) | async-done | bytes 9437200 | tf_op jit(solution)/shard_map/all_gather | solution.py:377
  2144.2 78.1 %all-gather.70.cloned.1.call-done = bf16[128,12,6448]{2,1,0:T(8,128)(2,1)} async-done(((bf16[1,12,6448]{2,1,0:T(8,128)(2,1)}), bf16[128,12,6448]{2,1,0:T(8,128)(2,1)}) %all-gather.70.cloned.1.call-update) | async-done | bytes 19808272 | tf_op jit(solution)/shard_map/all_gather | solution.py:376
  2309.5 53.5 %all-gather.72.cloned.1.call-done = bf16[128,12,1536]{2,1,0:T(8,128)(2,1)} async-done(((bf16[1,12,1536]{2,1,0:T(8,128)(2,1)}), bf16[128,12,1536]{2,1,0:T(8,128)(2,1)}) %all-gather.72.cloned.1.call-update) | async-done | bytes 4718608 | tf_op jit(solution)/shard_map/all_gather | solution.py:386
  2383.6 54.1 %all-gather.94.cloned.1.call-done = bf16[128,12,3072]{2,1,0:T(8,128)(2,1)} async-done(((bf16[1,12,3072]{2,1,0:T(8,128)(2,1)}), bf16[128,12,3072]{2,1,0:T(8,128)(2,1)}) %all-gather.94.cloned.1.call-update) | async-done | bytes 9437200 | tf_op jit(solution)/shard_map/all_gather | solution.py:377
  2458.5 78.3 %all-gather.74.cloned.1.call-done = bf16[128,12,6448]{2,1,0:T(8,128)(2,1)} async-done(((bf16[1,12,6448]{2,1,0:T(8,128)(2,1)}), bf16[128,12,6448]{2,1,0:T(8,128)(2,1)}) %all-gather.74.cloned.1.call-update) | async-done | bytes 19808272 | tf_op jit(solution)/shard_map/all_gather | solution.py:376
  2536.8 29.6 %reshape.464 = bf16[1536,6448]{1,0:T(8,128)(2,1)} reshape(bf16[128,12,6448]{2,1,0:T(8,128)(2,1)} %all-gather.74.cloned.1.call-done) | data formatting | bytes 39616512
  2624.0 53.6 %all-gather.76.cloned.1.call-done = bf16[128,12,1536]{2,1,0:T(8,128)(2,1)} async-done(((bf16[1,12,1536]{2,1,0:T(8,128)(2,1)}), bf16[128,12,1536]{2,1,0:T(8,128)(2,1)}) %all-gather.76.cloned.1.call-update) | async-done | bytes 4718608 | tf_op jit(solution)/shard_map/all_gather | solution.py:386
  (547 shorter events, 927.1 us)
Async XLA Ops:
  7.9 178.5 %all-gather.56.cloned.1.call-start = ((), (), s32[]{:S(2)}) async-start(), calls=%async_computation.3 | async-start | bytes 12681216 | tf_op jit(solution)/shard_map/all_gather | solution.py:250
  8.7 272.7 %all-gather.50.cloned.1.call-start = ((), (), s32[]{:S(2)}) async-start(), calls=%async_computation | async-start | bytes 25952256 | tf_op jit(solution)/shard_map/all_gather | solution.py:33
  179.8 266.8 %all-gather.52.cloned.1.call-start = ((), (), s32[]{:S(2)}) async-start(), calls=%async_computation.1 | async-start | bytes 25952256 | tf_op jit(solution)/shard_map/all_gather | solution.py:53
  309.4 722.5 %all-reduce.18.cloned.1.call-start = ((), (), s32[]{:S(2)}) async-start(), calls=%async_computation.24 | async-start | bytes 117153792
  648.2 532.2 %all-gather.78.cloned.1.call-start = ((), (), s32[]{:S(2)}) async-start(), calls=%async_computation.14 | async-start | bytes 12681216 | tf_op jit(solution)/shard_map/all_gather | solution.py:377
  1109.1 170.3 %all-gather.58.cloned.1.call-start = ((), (), s32[]{:S(2)}) async-start(), calls=%async_computation.4 | async-start | bytes 26947584 | tf_op jit(solution)/shard_map/all_gather | solution.py:376
  1110.6 240.1 %all-gather.80.cloned.1.call-start = ((), (), s32[]{:S(2)}) async-start(), calls=%async_computation.15 | async-start | bytes 6340608 | tf_op jit(solution)/shard_map/all_gather | solution.py:387
  1201.0 219.4 %all-gather.60.cloned.1.call-start = ((), (), s32[]{:S(2)}) async-start(), calls=%async_computation.5 | async-start | bytes 6340608 | tf_op jit(solution)/shard_map/all_gather | solution.py:386
  1321.5 173.4 %all-gather.82.cloned.1.call-start = ((), (), s32[]{:S(2)}) async-start(), calls=%async_computation.16 | async-start | bytes 12681216 | tf_op jit(solution)/shard_map/all_gather | solution.py:377
  1366.7 227.1 %all-gather.62.cloned.1.call-start = ((), (), s32[]{:S(2)}) async-start(), calls=%async_computation.6 | async-start | bytes 26947584 | tf_op jit(solution)/shard_map/all_gather | solution.py:376
  1440.8 224.2 %all-gather.84.cloned.1.call-start = ((), (), s32[]{:S(2)}) async-start(), calls=%async_computation.17 | async-start | bytes 6340608 | tf_op jit(solution)/shard_map/all_gather | solution.py:387
  1515.9 218.8 %all-gather.64.cloned.1.call-start = ((), (), s32[]{:S(2)}) async-start(), calls=%async_computation.7 | async-start | bytes 6340608 | tf_op jit(solution)/shard_map/all_gather | solution.py:386
  1636.0 173.2 %all-gather.86.cloned.1.call-start = ((), (), s32[]{:S(2)}) async-start(), calls=%async_computation.18 | async-start | bytes 12681216 | tf_op jit(solution)/shard_map/all_gather | solution.py:377
  1681.1 227.0 %all-gather.66.cloned.1.call-start = ((), (), s32[]{:S(2)}) async-start(), calls=%async_computation.8 | async-start | bytes 26947584 | tf_op jit(solution)/shard_map/all_gather | solution.py:376
  1755.2 224.1 %all-gather.88.cloned.1.call-start = ((), (), s32[]{:S(2)}) async-start(), calls=%async_computation.19 | async-start | bytes 6340608 | tf_op jit(solution)/shard_map/all_gather | solution.py:387
  1830.0 218.7 %all-gather.68.cloned.1.call-start = ((), (), s32[]{:S(2)}) async-start(), calls=%async_computation.9 | async-start | bytes 6340608 | tf_op jit(solution)/shard_map/all_gather | solution.py:386
  1950.2 173.1 %all-gather.90.cloned.1.call-start = ((), (), s32[]{:S(2)}) async-start(), calls=%async_computation.20 | async-start | bytes 12681216 | tf_op jit(solution)/shard_map/all_gather | solution.py:377
  1995.3 227.0 %all-gather.70.cloned.1.call-start = ((), (), s32[]{:S(2)}) async-start(), calls=%async_computation.10 | async-start | bytes 26947584 | tf_op jit(solution)/shard_map/all_gather | solution.py:376
  2069.2 224.2 %all-gather.92.cloned.1.call-start = ((), (), s32[]{:S(2)}) async-start(), calls=%async_computation.21 | async-start | bytes 6340608 | tf_op jit(solution)/shard_map/all_gather | solution.py:387
  2144.1 219.0 %all-gather.72.cloned.1.call-start = ((), (), s32[]{:S(2)}) async-start(), calls=%async_computation.11 | async-start | bytes 6340608 | tf_op jit(solution)/shard_map/all_gather | solution.py:386
  2264.4 173.4 %all-gather.94.cloned.1.call-start = ((), (), s32[]{:S(2)}) async-start(), calls=%async_computation.22 | async-start | bytes 12681216 | tf_op jit(solution)/shard_map/all_gather | solution.py:377
  2309.5 227.3 %all-gather.74.cloned.1.call-start = ((), (), s32[]{:S(2)}) async-start(), calls=%async_computation.12 | async-start | bytes 26947584 | tf_op jit(solution)/shard_map/all_gather | solution.py:376
  2383.6 224.4 %all-gather.96.cloned.1.call-start = ((), (), s32[]{:S(2)}) async-start(), calls=%async_computation.23 | async-start | bytes 6340608 | tf_op jit(solution)/shard_map/all_gather | solution.py:387
  2458.4 219.2 %all-gather.76.cloned.1.call-start = ((), (), s32[]{:S(2)}) async-start(), calls=%async_computation.13 | async-start | bytes 6340608 | tf_op jit(solution)/shard_map/all_gather | solution.py:386
  (130 other events, 4484.4 us)
Sparse Core Ops, SparseCore 0:
  11.1 99.4 all-gather.53
  113.7 72.7 all-gather.55
  189.3 92.0 all-gather.49
  309.5 137.0 all-gather.51
  648.3 383.5 all-reduce.17
  1109.2 71.0 all-gather.77
  1184.1 95.2 all-gather.57
  1283.1 67.6 all-gather.79
  1354.4 65.8 all-gather.59
  1423.9 70.9 all-gather.81
  1498.6 95.2 all-gather.61
  1597.4 67.6 all-gather.83
  1668.8 65.8 all-gather.63
  1738.2 70.9 all-gather.85
  1812.8 95.2 all-gather.65
  1911.6 67.6 all-gather.87
  1982.8 65.8 all-gather.67
  2052.3 70.9 all-gather.89
  2127.0 95.2 all-gather.69
  2225.8 67.6 all-gather.91
  2297.2 65.8 all-gather.71
  2366.8 70.9 all-gather.93
  2441.5 95.2 all-gather.73
  2540.3 67.6 all-gather.95
  (1 shorter events, 65.8 us)
where the time goes:
time: 2730 us; the launch traced here: 2710 us
  waiting for transfers between devices  1680 us (62%)
  local copies, waits for them, and re-layouts  392 us (14%)
  matrix products  315 us (12%)
  other arithmetic  158 us (6%)
  blocking collectives  129 us (5%)
    all_gather x5, waiting for transfers between devices, local(): lax.all_gather(low_in, ('fsdp', 'ctx'), axis=0, tiled=True)  391 us
    unnamed x26, waiting for transfers between devices  385 us
    unnamed x281, local copies, waits for them, and re-layouts  352 us
    all_gather x5, waiting for transfers between devices, local(): lax.all_gather(low_out, ('fsdp', 'ctx'), axis=0, tiled=True)  286 us
    all_gather x5, waiting for transfers between devices, local(): lax.all_gather(gram_in, ('fsdp', 'ctx'), axis=0, tiled=True)  268 us
    all_gather x5, waiting for transfers between devices, local(): lax.all_gather(gram_out, ('fsdp', 'ctx'), axis=0, tiled=True)  135 us
    all_gather x1, waiting for transfers between devices, entering_2(): lax.all_gather(part.astype(kind), axis)  114 us
    all_gather x1, waiting for transfers between devices, local(): lax.all_gather(in_weight, ('fsdp', 'ctx'), axis=0, tiled=True)  87.7 us
  transfers between devices with their start and end apart: 28, of which 26 were waited for; matrix products, arithmetic and copies ran while one was open for 23% of the time, Pallas kernels for 0%

commit v1 on v0

v1 whole, which is shorter than its diff:
```python
import math

import jax
import jax.numpy as jnp
from jax import lax
from jax.experimental import pallas as pl
from jax.experimental.pallas import tpu as pltpu
from jax.sharding import Mesh, PartitionSpec as P

NS_STEPS = 5
TWO_PART_STEPS = 2
CHUNK = 128
EPSILON = 1e-05
NORM_FLOOR = 1e-07
POLY_FIRST = 3.4445
POLY_SECOND = -4.775
POLY_THIRD = 2.0315
MATRIX_MOMENTUM = 0.95
MATRIX_RATE = 0.5
VECTOR_MOMENTUM = 0.9
VECTOR_RATE = 0.05
HIGHEST = lax.Precision.HIGHEST
F32 = jnp.float32
BF16 = jnp.bfloat16

EVERY = ("z", "x", "y", "c")
TEAM = ("y", "c")
ROWS = ("z", "x")

D = 1536
H = 48
HEAD = 64
N = 128
E = 3072
CH = 3328
PROJ = 6448
G = 8
HG = H // G
EG = E // G
BG = 2 * N // G
IN_COLS = 2 * EG + 128
OUT_COLS = EG
BLOCK = IN_COLS + OUT_COLS
FORWARD_COLS = 2 * EG + 2 * N + 128


def dot(a, b, dims):
    return lax.dot_general(
        a.astype(BF16), b.astype(BF16), (dims, ((), ())), preferred_element_type=F32
    )


def esum(spec, a, b):
    return jnp.einsum(spec, a.astype(BF16), b.astype(BF16), preferred_element_type=F32)


def spread(per_head):
    return jnp.repeat(per_head, HEAD, axis=-1)


def per_head_sum(values):
    return jnp.sum(values.reshape(values.shape[:-1] + (HG, HEAD)), axis=-1)


def gram_kernel(x_ref, g_ref):
    parts, n, _ = x_ref.shape
    tile = 256

    def rows(i, _):
        at = pl.ds(pl.multiple_of(i * tile, tile), tile)
        total = jnp.zeros((tile, n), F32)
        for p in range(parts):
            total = total + lax.dot_general(
                x_ref[p, at, :],
                x_ref[p],
                (((1,), (1,)), ((), ())),
                preferred_element_type=F32,
            )
        g_ref[at, :] = total
        return 0

    lax.fori_loop(0, n // tile, rows, 0)


def gram(x):
    n = x.shape[1]
    return pl.pallas_call(
        gram_kernel,
        out_shape=jax.ShapeDtypeStruct((n, n), F32),
        in_specs=[pl.BlockSpec(memory_space=pltpu.VMEM)],
        out_specs=pl.BlockSpec(memory_space=pltpu.VMEM),
        compiler_params=pltpu.CompilerParams(vmem_limit_bytes=48 << 20),
        cost_estimate=pl.CostEstimate(
            flops=2 * n * n * x.shape[0] * x.shape[2],
            bytes_accessed=2 * x.size + 4 * n * n,
            transcendentals=0,
        ),
        name="gram",
    )(x)


def chain_kernel(inverse_ref, g_ref, pick_ref, t_ref, high, low, h_high, h_low, q_ref):
    n = g_ref.shape[0]
    tile = 256
    inverse = inverse_ref[0]

    def at(i):
        return pl.ds(pl.multiple_of(i * tile, tile), tile)

    def parts(value):
        top = value.astype(BF16)
        return top, (value - top.astype(F32)).astype(BF16)

    def times(a, b):
        return jnp.dot(a, b, preferred_element_type=F32)

    def load(i, _):
        high[at(i), :], low[at(i), :] = parts(g_ref[at(i), :] * (inverse * inverse))
        return 0

    lax.fori_loop(0, n // tile, load, 0)
    for step in range(NS_STEPS):
        both = step < TWO_PART_STEPS
        q = q_ref.at[step]

        def polynomial(i, _):
            own = high[at(i), :]
            square = times(own, high[...])
            q[at(i), :] = (POLY_SECOND * own.astype(F32) + POLY_THIRD * square).astype(BF16)
            return 0

        lax.fori_loop(0, n // tile, polynomial, 0)
        if step == NS_STEPS - 1:
            break

        def left(i, _):
            own = q[at(i), :]
            value = times(own, high[...]) + POLY_FIRST * high[at(i), :].astype(F32)
            if both:
                value = value + times(own, low[...]) + POLY_FIRST * low[at(i), :].astype(F32)
                h_high[at(i), :], h_low[at(i), :] = parts(value)
            else:
                h_high[at(i), :] = value.astype(BF16)
            return 0

        lax.fori_loop(0, n // tile, left, 0)

        def right(i, _):
            own = h_high[at(i), :]
            value = times(own, q[...]) + POLY_FIRST * own.astype(F32)
            if both:
                rest = h_low[at(i), :]
                value = value + times(rest, q[...]) + POLY_FIRST * rest.astype(F32)
            if step + 1 < TWO_PART_STEPS:
                high[at(i), :], low[at(i), :] = parts(value)
            else:
                high[at(i), :] = value.astype(BF16)
            return 0

        lax.fori_loop(0, n // tile, right, 0)

    t = pick_ref[...]
    for step in reversed(range(NS_STEPS)):
        top, rest = parts(t)
        t = POLY_FIRST * t + times(top, q_ref[step]) + times(rest, q_ref[step])
    t_ref[...] = t * inverse


def chain(inverse, g, pick):
    n = g.shape[0]
    whole = pl.BlockSpec(memory_space=pltpu.VMEM)
    return pl.pallas_call(
        chain_kernel,
        out_shape=jax.ShapeDtypeStruct(pick.shape, F32),
        in_specs=[pl.BlockSpec(memory_space=pltpu.SMEM), whole, whole],
        out_specs=whole,
        scratch_shapes=[pltpu.VMEM((n, n), BF16)] * 4 + [pltpu.VMEM((NS_STEPS, n, n), BF16)],
        compiler_params=pltpu.CompilerParams(vmem_limit_bytes=60 << 20),
        cost_estimate=pl.CostEstimate(
            flops=34 * n * n * n, bytes_accessed=4 * n * n, transcendentals=0
        ),
        name="chain",
    )(inverse, g, pick)


def shift_all(value, axis, direction):
    size = lax.axis_size(axis)
    return [
        lax.ppermute(
            value,
            axis,
            [(s, s + direction * k) for s in range(size) if 0 <= s + direction * k < size],
        )
        for k in range(1, size)
    ]


def pack(state, gain):
    row = jnp.pad(gain, (0, N - HG))[None, :]
    return jnp.concatenate([state, jnp.pad(row, ((0, 7), (0, 0)))], axis=0)


def incoming_state(state, gain, direction):
    packed = shift_all(pack(state, gain), "x", direction)
    total = jnp.zeros_like(state)
    for arrived in reversed(packed):
        far_gain = spread(arrived[EG, :HG])
        total = arrived[:EG] + far_gain[:, None] * total
    return total


def blocks_of_columns(in_rows, out_rows):
    count = in_rows.shape[0]
    kind = in_rows.dtype
    z = in_rows[:, :E].reshape(count, G, EG)
    xs = in_rows[:, E : 2 * E].reshape(count, G, EG)
    bc = in_rows[:, 2 * E : 2 * E + 2 * N].reshape(count, G, BG)
    r = in_rows[:, 2 * E + 2 * N :].reshape(count, G, HG)
    fill = jnp.zeros((count, G, 128 - BG - HG), kind)
    out = out_rows.reshape(count, G, EG)
    return jnp.concatenate([z, xs, bc, r, fill, out], axis=2).transpose(1, 0, 2)


def rows_of_blocks(blocks):
    count = blocks.shape[1]
    b = blocks.transpose(1, 0, 2)
    pieces = [
        b[:, :, :EG].reshape(count, E),
        b[:, :, EG : 2 * EG].reshape(count, E),
        b[:, :, 2 * EG : 2 * EG + BG].reshape(count, 2 * N),
        b[:, :, 2 * EG + BG : 2 * EG + BG + HG].reshape(count, H),
    ]
    return jnp.concatenate(pieces, axis=1), b[:, :, IN_COLS:].reshape(count, E)


def local(
    hidden,
    segments,
    norm_gain,
    in_weight,
    conv_weight,
    conv_bias,
    dt_bias,
    a_log,
    skip_scale,
    gate_gain,
    out_weight,
    cotangent,
    in_momentum,
    out_momentum,
    vector_momentum,
):
    zi, xi, yi, ci = (lax.axis_index(a) for a in EVERY)
    team = yi * 2 + ci
    rows = hidden.shape[0]
    count = in_weight.shape[0]
    tokens = rows * G
    pieces = tokens // CHUNK

    def mine(values, width, start=0, axis=-1):
        return lax.dynamic_slice_in_dim(values, start + team * width, width, axis % values.ndim)

    hidden_team = lax.all_gather(hidden, TEAM, axis=0, tiled=True)
    z_w = in_weight[:, :E].reshape(count, G, EG)
    xs_w = in_weight[:, E : 2 * E].reshape(count, G, EG)
    bc_w = jnp.broadcast_to(in_weight[:, None, 2 * E : 2 * E + 2 * N], (count, G, 2 * N))
    r_w = jnp.pad(
        in_weight[:, 2 * E + 2 * N :].reshape(count, G, HG), ((0, 0), (0, 0), (0, 128 - HG))
    )
    out_w = out_weight.reshape(count, G, EG)
    sent = jnp.concatenate([z_w, xs_w, bc_w, r_w, out_w], axis=2).transpose(1, 0, 2)
    sent = jnp.concatenate(
        [
            sent,
            blocks_of_columns(in_momentum.astype(BF16), out_momentum.astype(BF16)),
        ],
        axis=2,
    )
    got = lax.all_to_all(sent, TEAM, 0, 0, tiled=True).reshape(G * count, -1)
    width = FORWARD_COLS + OUT_COLS
    momentum_block = got[:, width:].astype(F32)
    weights = lax.all_gather(got[:, :width], ROWS, axis=0, tiled=True)
    w_forward = weights[:, :FORWARD_COLS]
    w_out = weights[:, FORWARD_COLS:]
    w_own = jnp.concatenate(
        [
            weights[:, : 2 * EG],
            mine(weights[:, 2 * EG : 2 * EG + 2 * N], BG),
            weights[:, 2 * EG + 2 * N : 2 * EG + 2 * N + HG],
            jnp.zeros((D, 128 - BG - HG), BF16),
        ],
        axis=1,
    )
    q_team = lax.all_gather(cotangent, TEAM, axis=0, tiled=True)
    ids = lax.all_gather(segments, ("x",) + TEAM, axis=0, tiled=True)
    ids = lax.dynamic_slice_in_dim(
        jnp.pad(ids, (8, 8), constant_values=-1), xi * tokens, tokens + 16, 0
    )
    seg = ids[8 : 8 + tokens]
    edge_hidden = lax.ppermute(
        hidden_team[tokens - 8 :], "x", [(s, s + 1) for s in range(lax.axis_size("x") - 1)]
    )

    def normed_of(values):
        scale = lax.rsqrt(jnp.mean(values * values, axis=-1, keepdims=True) + EPSILON)
        return (values * scale * norm_gain).astype(BF16)

    normed = normed_of(hidden_team.astype(F32))
    projected = dot(normed, w_forward, ((1,), (0,)))
    edge = dot(normed_of(edge_hidden.astype(F32)), w_forward[:, EG : 2 * EG + 2 * N], ((1,), (0,)))
    z = projected[:, :EG]
    conv_in = projected[:, EG : 2 * EG + 2 * N]
    r = projected[:, 2 * EG + 2 * N : 2 * EG + 2 * N + HG]

    taps = conv_weight.shape[0]
    tap_own = jnp.concatenate([mine(conv_weight[:, :E], EG), conv_weight[:, E:]], axis=1)
    bias_own = jnp.concatenate([mine(conv_bias[:E], EG), conv_bias[E:]])
    extended = jnp.concatenate([edge, conv_in], axis=0)
    conv = jnp.zeros_like(conv_in) + bias_own[None, :]
    for lag in range(taps):
        same = (ids[8 - lag : 8 - lag + tokens] == seg).astype(F32)
        conv = conv + tap_own[lag][None, :] * extended[8 - lag : 8 - lag + tokens] * same[:, None]
    act = jax.nn.silu(conv)
    xs = act[:, :EG]
    bm = act[:, EG : EG + N].reshape(pieces, CHUNK, N)
    cm = act[:, EG + N :].reshape(pieces, CHUNK, N)
    dt_shift = mine(dt_bias, HG)
    rate = jnp.exp(mine(a_log, HG))
    skip = mine(skip_scale, HG)
    dt = jax.nn.softplus(r + dt_shift[None, :])
    la = -rate[None, :] * dt

    def chunked(values):
        return values.reshape((pieces, CHUNK) + values.shape[1:])

    seg_c = chunked(seg)
    before = chunked(ids[7 : 7 + tokens])[:, 0]
    dt_c, la_c = chunked(dt), chunked(la)
    xs_c = chunked(xs)
    ti = lax.broadcasted_iota(jnp.int32, (CHUNK, CHUNK), 0)
    si = lax.broadcasted_iota(jnp.int32, (CHUNK, CHUNK), 1)
    lower = (ti >= si).astype(F32)
    cum = jnp.einsum("ts,csh->cth", lower, la_c, precision=HIGHEST)
    cum_h = cum.transpose(0, 2, 1)
    dt_h = dt_c.transpose(0, 2, 1)
    mask = (ti >= si)[None] & (seg_c[:, :, None] == seg_c[:, None, :])
    gap = cum_h[:, :, :, None] - cum_h[:, :, None, :]
    decay = jnp.exp(jnp.where(mask[:, None], gap, -1e30))
    scores = esum("ctn,csn->cts", cm, bm)
    mixing = (decay * scores[:, None]).astype(BF16)
    xs_heads = xs_c.reshape(pieces, CHUNK, HG, HEAD)
    xdt = xs_c * spread(dt_c)
    xdt_heads = xdt.reshape(pieces, CHUNK, HG, HEAD)
    within = esum("chts,cshp->cthp", mixing, xdt_heads).reshape(pieces, CHUNK, EG)
    keep = (seg_c == before[:, None]).astype(F32)
    last = cum[:, -1]
    tail = jnp.exp(last[:, None] - cum) * (seg_c == seg_c[:, -1:]).astype(F32)[:, :, None]
    tail_wide = spread(tail)
    x_tail = (xdt * tail_wide).astype(BF16)
    fresh = esum("csp,csn->cpn", x_tail, bm)
    gain = jnp.exp(last) * (seg_c[:, -1] == before).astype(F32)[:, None]
    gain_wide = spread(gain)
    starts = [jnp.zeros((EG, N), F32)]
    reach = [jnp.ones((HG,), F32)]
    for p in range(pieces):
        starts.append(gain_wide[p][:, None] * starts[-1] + fresh[p])
        reach.append(gain[p] * reach[-1])
    arrived = incoming_state(starts[-1], reach[-1], 1)
    states = jnp.stack([s + spread(g)[:, None] * arrived for s, g in zip(starts, reach)])
    carry_gain = spread(jnp.exp(cum) * keep[:, :, None])
    carried = esum("ctn,cpn->ctp", cm, states[:pieces]) * carry_gain
    y_part = (within + carried).reshape(tokens, EG)
    skip_wide = spread(skip)
    y = y_part + skip_wide * xs

    d_gated = dot(q_team, w_out, ((1,), (0,)))
    gate_own = mine(gate_gain, EG)
    sig_z = jax.nn.sigmoid(z)
    silu_z = z * sig_z
    g = y * silu_z
    d_scaled = d_gated * gate_own
    sums = lax.psum(
        jnp.stack([jnp.sum(g * g, axis=1), jnp.sum(d_scaled * g, axis=1)]).reshape(-1, 128), TEAM
    ).reshape(2, tokens)
    root = lax.rsqrt(sums[0] / E + EPSILON)
    slope = sums[1] * root * root * root / E
    unit = g * root[:, None]
    gated = (unit * gate_own).astype(BF16)
    mixed = lax.psum_scatter(
        dot(gated, w_out, ((1,), (1,))), TEAM, scatter_dimension=0, tiled=True
    )
    hidden_own = hidden.astype(F32)
    block_output = (hidden_own + mixed).astype(BF16)
    out_partial = dot(q_team, gated, ((0,), (0,)))
    out_sum = lax.psum_scatter(out_partial, ROWS, scatter_dimension=0, tiled=True)
    d_gate_gain = jnp.sum(d_gated * unit, axis=0)
    d_g = root[:, None] * d_scaled - g * slope[:, None]
    d_y = d_g * silu_z
    d_z = d_g * y * (sig_z + silu_z * (1.0 - sig_z))

    dy_c = chunked(d_y)
    dy_low = dy_c.astype(BF16)
    dy_heads = dy_low.reshape(pieces, CHUNK, HG, HEAD)
    dy_carry = (dy_c * carry_gain).astype(BF16)
    back = esum("ctp,ctn->cpn", dy_carry, cm)
    ends = [jnp.zeros((EG, N), F32)]
    reach_back = [jnp.ones((HG,), F32)]
    for p in reversed(range(pieces)):
        ends.append(back[p] + gain_wide[p][:, None] * ends[-1])
        reach_back.append(gain[p] * reach_back[-1])
    adjoint_in = incoming_state(ends[-1], reach_back[-1], -1)
    adjoints = jnp.stack(
        [s + spread(w)[:, None] * adjoint_in for s, w in zip(ends, reach_back)][:pieces][::-1]
    )
    u_intra = esum("chts,cthp->cshp", mixing, dy_heads).reshape(pieces, CHUNK, EG)
    u = u_intra + esum("csn,cpn->csp", bm, adjoints) * tail_wide
    d_xs = (u * spread(dt_c) + skip_wide * dy_c).reshape(tokens, EG)
    d_dt = per_head_sum(xs_c * u)
    pair = esum("cthp,cshp->chts", dy_heads, xdt_heads)
    d_scores = jnp.sum(decay * pair, axis=1)
    d_bm = esum("cts,ctn->csn", d_scores, cm) + esum("csp,cpn->csn", x_tail, adjoints)
    d_cm = esum("cts,csn->ctn", d_scores, bm) + esum("ctp,cpn->ctn", dy_carry, states[:pieces])
    ends_inner = jnp.sum(
        (adjoints * states[1:]).reshape(pieces, HG, HEAD * N), axis=2
    )
    flow = per_head_sum(dy_c * chunked(y_part)) - dt_c * d_dt
    upper = (si >= ti).astype(F32)
    d_la = jnp.einsum("ts,csh->cth", upper, flow, precision=HIGHEST) + ends_inner[:, None]
    linked = (ids[7 : 7 + tokens] == seg).astype(F32)
    d_la = d_la.reshape(tokens, HG) * linked[:, None]
    d_dt = d_dt.reshape(tokens, HG)
    d_skip = jnp.sum(per_head_sum(d_y * xs), axis=0)
    d_r = (d_dt - rate[None, :] * d_la) * jax.nn.sigmoid(r + dt_shift[None, :])
    d_dt_bias = jnp.sum(d_r, axis=0)
    d_a_log = jnp.sum(d_la * la, axis=0)

    d_bc = jnp.concatenate([d_bm, d_cm], axis=2).reshape(tokens, 2 * N).T
    d_bc = lax.all_to_all(d_bc.reshape(G, BG, tokens), TEAM, 0, 0, tiled=True)
    d_bc = jnp.sum(d_bc, axis=0).T
    conv_own = jnp.concatenate([conv[:, :EG], mine(conv[:, EG:], BG)], axis=1)
    ext_own = jnp.concatenate([extended[:, :EG], mine(extended[:, EG:], BG)], axis=1)
    tap_mine = jnp.concatenate([tap_own[:, :EG], mine(tap_own[:, EG:], BG)], axis=1)
    sig_c = jax.nn.sigmoid(conv_own)
    d_conv = jnp.concatenate([d_xs, d_bc], axis=1) * (sig_c + conv_own * sig_c * (1.0 - sig_c))
    next_conv = lax.ppermute(
        d_conv[:8], "x", [(s, s - 1) for s in range(1, lax.axis_size("x"))]
    )
    d_ext = jnp.concatenate([d_conv, next_conv], axis=0)
    d_v = jnp.zeros_like(d_conv)
    d_taps = []
    for lag in range(taps):
        ahead = (ids[8 + lag : 8 + lag + tokens] == seg).astype(F32)
        d_v = d_v + tap_mine[lag][None, :] * d_ext[lag : lag + tokens] * ahead[:, None]
        same = (ids[8 - lag : 8 - lag + tokens] == seg).astype(F32)
        d_taps.append(
            jnp.sum(d_conv * ext_own[8 - lag : 8 - lag + tokens] * same[:, None], axis=0)
        )
    d_bias = jnp.sum(d_conv, axis=0)
    d_projected = jnp.concatenate(
        [d_z, d_v, d_r, jnp.zeros((tokens, 128 - BG - HG), F32)], axis=1
    ).astype(BF16)
    in_partial = dot(normed, d_projected, ((0,), (0,)))
    in_parts = lax.all_to_all(
        in_partial.astype(BF16).reshape(16, G * count, IN_COLS), ROWS, 0, 0, tiled=True
    )
    in_sum = jnp.sum(in_parts.astype(F32), axis=0)
    d_normed = lax.psum_scatter(
        dot(d_projected, w_own, ((1,), (1,))), TEAM, scatter_dimension=0, tiled=True
    )
    scale_own = lax.rsqrt(jnp.mean(hidden_own * hidden_own, axis=-1, keepdims=True) + EPSILON)
    unit_own = hidden_own * scale_own
    d_unit = d_normed * norm_gain
    d_hidden = scale_own * (
        d_unit - unit_own * jnp.mean(d_unit * unit_own, axis=-1, keepdims=True)
    )
    input_grad = cotangent.astype(F32) + d_hidden
    d_norm_gain = jnp.sum(d_normed * unit_own, axis=0)

    def wide(values):
        return lax.all_gather(values.astype(BF16), ("y", "z", "x")).reshape(4, D, -1)

    x_out = wide(MATRIX_MOMENTUM * momentum_block[:, IN_COLS:] + out_sum)
    x_in = wide(MATRIX_MOMENTUM * momentum_block[:, :IN_COLS] + in_sum)
    gram_out = gram(x_out)
    gram_in = gram(x_in)
    swap = [(0, 1), (1, 0)]
    first = ci == 0
    other = lax.ppermute(jnp.where(first, gram_out, gram_in), "c", swap)
    gram_own = jnp.where(first, gram_in, gram_out) + other
    diagonal = lax.broadcasted_iota(jnp.int32, (D, D), 0) == lax.broadcasted_iota(
        jnp.int32, (D, D), 1
    )
    square = jnp.sum(jnp.where(diagonal, gram_own, 0.0))
    inverse = 1.0 / (jnp.sqrt(square) + NORM_FLOOR)
    chip_row = (zi * 4 + xi) * (G * count) + yi * (2 * count)
    pick = (
        lax.broadcasted_iota(jnp.int32, (2 * count, D), 1)
        == lax.broadcasted_iota(jnp.int32, (2 * count, D), 0) + chip_row
    ).astype(F32)
    t_own = chain(inverse.reshape(1), gram_own, pick)
    t_other = lax.ppermute(t_own, "c", swap)
    t_in = jnp.where(first, t_own, t_other)
    t_out = jnp.where(first, t_other, t_own)

    def applied(t, x):
        top = t.astype(BF16)
        rest = (t - top.astype(F32)).astype(BF16)
        both = esum("rk,ykn->yrn", jnp.concatenate([top, rest], axis=0), x)
        return both[:, : 2 * count] + both[:, 2 * count :]

    halves = jnp.concatenate([applied(t_in, x_in), applied(t_out, x_out)], axis=2)
    half_own = lax.dynamic_slice_in_dim(halves, ci * count, count, 1)
    half_sent = lax.dynamic_slice_in_dim(halves, (1 - ci) * count, count, 1)
    half_got = lax.ppermute(half_sent, "c", swap)
    both = jnp.stack(
        [jnp.where(first, half_own, half_got), jnp.where(first, half_got, half_own)], axis=1
    ).reshape(G, count, BLOCK)
    step_in, step_out = rows_of_blocks(both)
    in_weight_new = in_weight.astype(F32) - MATRIX_RATE * math.sqrt(PROJ / D) * step_in
    out_weight_new = out_weight.astype(F32) - MATRIX_RATE * math.sqrt(E / D) * step_out

    sums_block = jnp.concatenate([in_sum, out_sum], axis=1).reshape(G, count, BLOCK)
    in_grad, out_grad = rows_of_blocks(lax.all_to_all(sums_block, TEAM, 0, 0, tiled=True))
    in_momentum_new = MATRIX_MOMENTUM * in_momentum + in_grad
    out_momentum_new = MATRIX_MOMENTUM * out_momentum + out_grad

    vector = jnp.concatenate(
        [d_norm_gain, jnp.concatenate(d_taps), d_bias, d_gate_gain, d_dt_bias, d_a_log, d_skip]
    )
    vector = jnp.pad(vector, (0, -vector.shape[0] % 1024)).reshape(-1, 128)
    vector = jnp.sum(lax.all_gather(vector, ROWS), axis=0)
    vector = lax.all_gather(vector, TEAM).reshape(G, -1)
    own = EG + BG
    grad_gain = jnp.sum(vector[:, :D], axis=0)
    conv_parts = vector[:, D : D + (taps + 1) * own].reshape(G, taps + 1, own).transpose(1, 0, 2)
    conv_parts = jnp.concatenate(
        [
            conv_parts[:, :, :EG].reshape(taps + 1, E),
            conv_parts[:, :, EG:].reshape(taps + 1, 2 * N),
        ],
        axis=1,
    )
    rest = vector[:, D + (taps + 1) * own :]
    heads = rest[:, EG : EG + 3 * HG].reshape(G, 3, HG).transpose(1, 0, 2).reshape(-1)
    vector_grad = jnp.concatenate(
        [grad_gain, conv_parts.reshape(-1), heads, rest[:, :EG].reshape(-1)]
    )
    vector_old = jnp.concatenate(
        [norm_gain, conv_weight.reshape(-1), conv_bias, dt_bias, a_log, skip_scale, gate_gain]
    )
    vector_momentum_new = VECTOR_MOMENTUM * vector_momentum + (1.0 - VECTOR_MOMENTUM) * vector_grad
    vector_new = vector_old - VECTOR_RATE * vector_momentum_new
    return (
        block_output,
        input_grad,
        in_grad,
        in_momentum_new,
        in_weight_new,
        out_grad,
        out_momentum_new,
        out_weight_new,
        vector_grad,
        vector_momentum_new,
        vector_new,
    )


def solution(mesh):
    grid = Mesh(mesh.devices.reshape(4, 4, 4, 2), EVERY)
    split = P(EVERY, None)
    return jax.shard_map(
        local,
        mesh=grid,
        in_specs=(
            split,
            P(EVERY),
            P(),
            split,
            P(),
            P(),
            P(),
            P(),
            P(),
            P(),
            split,
            split,
            split,
            split,
            P(),
        ),
        out_specs=(split,) * 8 + (P(),) * 3,
        check_vma=False,
    )
```

time: 2730 us -> 783 us (0.29)
  waiting for transfers between devices: 1680 us -> 134 us
  local copies, waits for them, and re-layouts: 392 us -> 83 us
  matrix products: 315 us -> 65.2 us
  Pallas kernels: 0 us -> 199 us
  other arithmetic: 158 us -> 93.8 us
  starting transfers between devices: 11.4 us -> 41.4 us
    all_gather x24 -> x5, waiting for transfers between devices: 1290 us -> 92 us  [the longest x2 59.1 us: wide(): lax.all_gather(values.astype(BF16), ('y', 'z', 'x')).reshape(4, D, -1)]
    unnamed x26 -> x8, waiting for transfers between devices: 385 us -> 1.46 us
    unnamed x281 -> x397, local copies, waits for them, and re-layouts: 352 us -> 18.7 us
    dot_general x42 -> x23, matrix products: 315 us -> 65.2 us  [the longest x7 37.2 us: dot(): lax.dot_general(a.astype(BF16), b.astype(BF16), (dims, ((), ())), preferr...]
    pallas_call x0 -> x3, Pallas kernels: none -> 199 us  [the longest x1 156 us: chain(): pl.pallas_call(chain_kernel, out_shape=jax.ShapeDtypeStruct(pick.shape, F...]
    all_to_all x0 -> x2, blocking collectives: none -> 65.6 us  [the longest x1 47 us: local(): lax.all_to_all(in_partial.astype(BF16).reshape(16, G * count, IN_COLS), R...]
    unnamed x1 -> x0, blocking collectives: 63.8 us -> none
    all_gather x0 -> x3, blocking collectives: none -> 59.4 us  [the longest x1 22.2 us: local(): ids = lax.all_gather(segments, ('x',) + TEAM, axis=0, tiled=True)]
  transfers between devices with their start and end apart: 28 -> 21, of which waited for: 26 -> 7; matrix products, arithmetic and copies ran while one was open for 23% -> 27% of each run, Pallas kernels for 0% -> 26%
where the time goes in v1:
time: 783 us; the launch traced here: 773 us
  Pallas kernels  199 us (25%)
  blocking collectives  138 us (18%)
  waiting for transfers between devices  134 us (17%)
  other arithmetic  93.8 us (12%)
  local copies, waits for them, and re-layouts  83 us (11%)
  matrix products  65.2 us (8%)
  starting transfers between devices  41.4 us (5%)
  between operations  18.1 us (2%)
    pallas_call x1, Pallas kernels, chain(): pl.pallas_call(chain_kernel, out_shape=jax.ShapeDtypeStruct(pick.shape, F...  156 us
    all_gather x2, waiting for transfers between devices, wide(): lax.all_gather(values.astype(BF16), ('y', 'z', 'x')).reshape(4, D, -1)  59.1 us
    all_to_all x1, blocking collectives, local(): lax.all_to_all(in_partial.astype(BF16).reshape(16, G * count, IN_COLS), R...  47 us
    pallas_call x2, Pallas kernels, gram(): pl.pallas_call(gram_kernel, out_shape=jax.ShapeDtypeStruct((n, n), F32),...  42.7 us
    dot_general x7, matrix products, dot(): lax.dot_general(a.astype(BF16), b.astype(BF16), (dims, ((), ())), preferr...  37.2 us
    all_gather x1, waiting for transfers between devices, local(): weights = lax.all_gather(got[:, :width], ROWS, axis=0, tiled=True)  32.9 us
    reduce_scatter x1, waiting for transfers between devices, local(): lax.psum_scatter(out_partial, ROWS, scatter_dimension=0, tiled=True)  29.2 us
    dot_general x14, matrix products, esum(): jnp.einsum(spec, a.astype(BF16), b.astype(BF16), preferred_element_type=F32)  27.6 us
  transfers between devices with their start and end apart: 21, of which 7 were waited for; matrix products, arithmetic and copies ran while one was open for 27% of the time, Pallas kernels for 26%

profile of v1, /device:TPU:1, one launch (start us, length us, event | category | flops | bytes accessed | tf_op | source)
XLA Modules:
  0.0 772.6 jit_solution(11420162281165689385)
XLA Ops:
  10.2 18.6 %all_to_all.20 = bf16[8,12,2816]{2,1,0:T(8,128)(2,1)S(1)} all-to-all(bf16[8,12,2816]{2,1,0:T(8,128)(2,1)S(1)} %pad_maximum_fusion.4), channel_id=1, replica_groups=mesh['z'=4,'x'=4,'y'=4,'c'=2] {'y','c'}, dimensions={0} | all-to-all | bytes 1081344 | tf_op jit(solution)/shard_map/all_to_all | solution.py:279
  30.6 22.2 %all-gather.3 = s32[32,1,128]{2,1,0:T(1,128)S(1)} all-gather(s32[1,1,128]{2,1,0:T(1,128)S(1)} %bitcast.521), channel_id=1, replica_groups=mesh['z'=4,'x'=4,'y'=4,'c'=2] {'x','y','c'}, dimensions={0}, use_global_device_ids=true | all-gather | bytes 16896 | tf_op jit(solution)/shard_map/all_gather | solution.py:295
  66.6 32.9 %all-gather.12.cloned.1.call-done = bf16[1536,1536]{1,0:T(8,128)(2,1)} async-done(((bf16[96,1536]{1,0:T(8,128)(2,1)}), bf16[1536,1536]{1,0:T(8,128)(2,1)}) %all-gather.12.cloned.1.call-update) | async-done | bytes 4718608 | tf_op jit(solution)/shard_map/all_gather | solution.py:282
  99.5 6.3 fusion.3
  185.0 7.0 multiply_reduce_fusion.4
  192.0 13.2 %psum.7 = f32[16,128]{1,0:T(8,128)S(1)} all-reduce(f32[16,128]{1,0:T(8,128)S(1)} %reshape.422), channel_id=1, replica_groups=mesh['z'=4,'x'=4,'y'=4,'c'=2] {'y','c'}, use_global_device_ids=true, to_apply=%region_4.5 | all-reduce | flops 2048 | bytes 16384 | tf_op jit(solution)/shard_map/psum | solution.py:382
  213.8 5.3 multiply_reduce_fusion.1
  227.4 12.0 %collective-permute-start.4 = (f32[392,128]{1,0:T(8,128)}, f32[392,128]{1,0:T(8,128)}, u32[]{:S(2)}, u32[]{:S(2)}) collective-permute-start(f32[392,128]{1,0:T(8,128)} %select_maximum_fusion), channel_id=1, source_target_pairs={{8,0},{16,8},{24,16},{9,1},{17,9},{25,17},{10,2},{18,10},{26,18},{... | collective-permute-start | bytes 602120 | tf_op jit(solution)/shard_map/ppermute | solution.py:189
  257.7 29.2 %reduce-scatter.10.cloned.1.call-done = f32[96,384]{1,0:T(8,128)} async-done(((f32[1536,384]{1,0:T(8,128)}), f32[96,384]{1,0:T(8,128)}) %reduce-scatter.10.cloned.1.call-update) | async-done | bytes 147472 | tf_op jit(solution)/shard_map/reduce_scatter | solution.py:395
  300.5 6.6 all-to-all-start.1
  307.1 6.1 multiply_add_fusion
  324.2 5.7 fusion.47
  342.4 47.0 %all_to_all.21 = bf16[16,96,896]{2,1,0:T(8,128)(2,1)S(1)} all-to-all(bf16[16,96,896]{2,1,0:T(8,128)(2,1)S(1)} %bitcast.468), channel_id=1, replica_groups=mesh['z'=4,'x'=4,'y'=4,'c'=2] {'z','x'}, dimensions={0} | all-to-all | bytes 5505024 | tf_op jit(solution)/shard_map/all_to_all | solution.py:463
  394.2 6.1 fusion.5
  402.8 14.5 %gram.3 = f32[1536,1536]{1,0:T(8,128)} custom-call(bf16[4,1536,384]{2,1,0:T(8,128)(2,1)S(1)} %bitcast.439), custom_call_target="tpu_custom_call" | custom-call | flops 7247757312 | bytes 14155776 | tf_op jit(solution)/shard_map/gram/pallas_call | solution.py:87
  417.3 59.1 %all-gather.16.cloned.1.call-done = bf16[6144,896]{1,0:T(8,128)(2,1)} async-done(((bf16[96,896]{1,0:T(8,128)(2,1)}), bf16[6144,896]{1,0:T(8,128)(2,1)}) %all-gather.16.cloned.1.call-update) | async-done | bytes 11010064 | tf_op jit(solution)/shard_map/all_gather | solution.py:480
  476.4 28.2 %gram.2 = f32[1536,1536]{1,0:T(8,128)} custom-call(bf16[4,1536,896]{2,1,0:T(8,128)(2,1)} %bitcast.444), custom_call_target="tpu_custom_call" | custom-call | flops 16911433728 | bytes 20447232 | tf_op jit(solution)/shard_map/gram/pallas_call | solution.py:87
  504.7 9.8 %broadcast_select_fusion = f32[1536,1536]{1,0:T(8,128)} fusion(f32[1536,1536]{1,0:T(8,128)} %gram.3, f32[1536,1536]{1,0:T(8,128)} %gram.2, pred[]{:T(512)S(6)} %eq.96), kind=kLoop, calls=%fused_computation.13 | loop fusion | flops 2359296 | bytes 28311552 | tf_op jit(solution)/shard_map/jit(_where)/select_n | solution.py:488
  521.8 5.7 fusion.71
  536.9 20.1 %all_gather.41 = f32[16,32,128]{2,1,0:T(8,128)S(1)} all-gather(f32[1,32,128]{2,1,0:T(8,128)S(1)} %pad_bitcast_fusion), channel_id=1, replica_groups=mesh['z'=4,'x'=4,'y'=4,'c'=2] {'z','x'}, dimensions={0}, use_global_device_ids=true | all-gather | bytes 278528 | tf_op jit(solution)/shard_map/all_gather | solution.py:531
  557.1 17.0 %all-gather.2 = f32[256,128]{1,0:T(8,128)S(1)} all-gather(f32[32,128]{1,0:T(8,128)S(1)} %reduce_sum.270), channel_id=4, replica_groups=mesh['z'=4,'x'=4,'y'=4,'c'=2] {'y','c'}, dimensions={0}, use_global_device_ids=true | all-gather | bytes 147456 | tf_op jit(solution)/shard_map/all_gather | solution.py:532
  575.6 12.7 %select_reduce_fusion = (f32[]{:T(128)}, f32[1536,1536]{1,0:T(8,128)}) fusion(f32[1536,1536]{1,0:T(8,128)} %collective-permute-done.8, f32[1536,1536]{1,0:T(8,128)} %gram.2, f32[1536,1536]{1,0:T(8,128)} %gram.3, pred[]{:T(512)S(6)} %eq.96), kind=kLoop, calls=%fused_computation | loop fusion | flops 11796479 | bytes 37748740 | tf_op jit(solution)/shard_map/reduce_sum | solution.py:493
  589.1 156.4 %chain.1 = f32[24,1536]{1,0:T(8,128)} custom-call(f32[1]{0:T(128)} %bitcast.96.inverse_ref, f32[1536,1536]{1,0:T(8,128)} %get-tuple-element.32.g_ref, f32[24,1536]{1,0:T(8,128)} %fusion.128.pick_ref), custom_call_target="tpu_custom_call" | custom-call | flops 123211874304 | bytes 9437184 | tf_op jit(solution)/shard_map/chain/pallas_call | solution.py:172
  752.5 6.1 convolution_bitcast_fusion.1
  (739 shorter events, 206.5 us)
Async XLA Ops:
  7.2 52.9 %all-gather.10.cloned.1.call-start = ((), (), s32[]{:S(2)}) async-start(), calls=%async_computation.7 | async-start | bytes 3538944 | tf_op jit(solution)/shard_map/all_gather | solution.py:263
  8.0 91.6 %all-gather.12.cloned.1.call-start = ((), (), s32[]{:S(2)}) async-start(), calls=%async_computation.8 | async-start | bytes 5013504 | tf_op jit(solution)/shard_map/all_gather | solution.py:282
  29.7 155.3 %all-gather.14.cloned.1.call-start = ((), (), s32[]{:S(2)}) async-start(), calls=%async_computation.9 | async-start | bytes 3538944 | tf_op jit(solution)/shard_map/all_gather | solution.py:294
  30.5 256.4 %reduce-scatter.10.cloned.1.call-start = ((), (), s32[]{:S(2)}) async-start(), calls=%async_computation.14 | async-start | bytes 2506752 | tf_op jit(solution)/shard_map/reduce_scatter | solution.py:395
  54.8 53.7 %copy-start.154 = (f32[6]{0:T(128)}, f32[6]{0:T(128)S(1)}, u32[]{:S(2)}) copy-start(f32[6]{0:T(128)S(1)} %dynamic_slice.42) | copy-start | bytes 76
  61.0 5.5 collective-permute-start
  115.3 68.8 %copy-start.20 = (bf16[1024,128]{1,0:T(8,128)(2,1)}, bf16[1024,128]{1,0:T(8,128)(2,1)S(1)}, u32[]{:S(2)}) copy-start(bf16[1024,128]{1,0:T(8,128)(2,1)S(1)} %get-tuple-element.74) | copy-start | bytes 786436
  121.3 60.5 %copy-start.90 = (f32[384]{0:T(512)}, f32[384]{0:T(512)S(1)}, u32[]{:S(2)}) copy-start(f32[384]{0:T(512)S(1)} %broadcast_in_dim.201) | copy-start | bytes 4612
  141.8 35.3 %collective-permute-start.3 = (f32[392,128]{1,0:T(8,128)}, f32[392,128]{1,0:T(8,128)}, u32[]{:S(2)}, u32[]{:S(2)}) collective-permute-start(f32[392,128]{1,0:T(8,128)} %select_maximum_fusion.1), channel_id=1, source_target_pairs={{0,24},{1,25},{2,26},{3,27},{4,28},{5,29},{6,30},{7,31},{32,56},{3... | collective-permute-start | bytes 602120 | tf_op jit(solution)/shard_map/ppermute | solution.py:189
  146.8 31.1 %collective-permute-start.2 = (f32[392,128]{1,0:T(8,128)}, f32[392,128]{1,0:T(8,128)}, u32[]{:S(2)}, u32[]{:S(2)}) collective-permute-start(f32[392,128]{1,0:T(8,128)} %select_maximum_fusion.1), channel_id=1, source_target_pairs={{0,16},{8,24},{1,17},{9,25},{2,18},{10,26},{3,19},{11,27},{4,20},{... | collective-permute-start | bytes 602120 | tf_op jit(solution)/shard_map/ppermute | solution.py:189
  148.7 30.0 %collective-permute-start.1 = (f32[392,128]{1,0:T(8,128)}, f32[392,128]{1,0:T(8,128)}, u32[]{:S(2)}, u32[]{:S(2)}) collective-permute-start(f32[392,128]{1,0:T(8,128)} %select_maximum_fusion.1), channel_id=1, source_target_pairs={{0,8},{8,16},{16,24},{1,9},{9,17},{17,25},{2,10},{10,18},{18,26},{... | collective-permute-start | bytes 602120 | tf_op jit(solution)/shard_map/ppermute | solution.py:189
  213.2 187.2 %all-gather.18.cloned.1.call-start = ((), (), s32[]{:S(2)}) async-start(), calls=%async_computation.13 | async-start | bytes 4792320 | tf_op jit(solution)/shard_map/all_gather | solution.py:480
  224.8 63.7 %collective-permute-start.6 = (f32[392,128]{1,0:T(8,128)}, f32[392,128]{1,0:T(8,128)}, u32[]{:S(2)}, u32[]{:S(2)}) collective-permute-start(f32[392,128]{1,0:T(8,128)} %select_maximum_fusion), channel_id=1, source_target_pairs={{24,0},{25,1},{26,2},{27,3},{28,4},{29,5},{30,6},{31,7},{56,32},{5... | collective-permute-start | bytes 602120 | tf_op jit(solution)/shard_map/ppermute | solution.py:189
  226.1 63.2 %collective-permute-start.5 = (f32[392,128]{1,0:T(8,128)}, f32[392,128]{1,0:T(8,128)}, u32[]{:S(2)}, u32[]{:S(2)}) collective-permute-start(f32[392,128]{1,0:T(8,128)} %select_maximum_fusion), channel_id=1, source_target_pairs={{16,0},{24,8},{17,1},{25,9},{18,2},{26,10},{19,3},{27,11},{20,4},{... | collective-permute-start | bytes 602120 | tf_op jit(solution)/shard_map/ppermute | solution.py:189
  227.4 62.8 %collective-permute-start.4 = (f32[392,128]{1,0:T(8,128)}, f32[392,128]{1,0:T(8,128)}, u32[]{:S(2)}, u32[]{:S(2)}) collective-permute-start(f32[392,128]{1,0:T(8,128)} %select_maximum_fusion), channel_id=1, source_target_pairs={{8,0},{16,8},{24,16},{9,1},{17,9},{25,17},{10,2},{18,10},{26,18},{... | collective-permute-start | bytes 602120 | tf_op jit(solution)/shard_map/ppermute | solution.py:189
  300.5 22.1 %all-to-all-start.1 = ((f32[8,32,1024]{2,1,0:T(8,128)}), f32[8,32,1024]{2,1,0:T(8,128)}, u32[]{:S(2)}, u32[]{:S(2)}) async-start(f32[8,32,1024]{2,1,0:T(8,128)} %bitcast.462), calls=%async_computation.2 | async-start | bytes 2097152 | tf_op jit(solution)/shard_map/all_to_all | solution.py:438
  307.1 169.3 %all-gather.16.cloned.1.call-start = ((), (), s32[]{:S(2)}) async-start(), calls=%async_computation.12 | async-start | bytes 11182080 | tf_op jit(solution)/shard_map/all_gather | solution.py:480
  330.0 5.0 collective-permute-start.7
  391.2 144.1 %reduce-scatter.8.cloned.1.call-start = ((), (), s32[]{:S(2)}) async-start(), calls=%async_computation.11 | async-start | bytes 7077888 | tf_op jit(solution)/shard_map/reduce_scatter | solution.py:467
  514.5 61.1 %collective-permute-start.8 = (f32[1536,1536]{1,0:T(8,128)}, f32[1536,1536]{1,0:T(8,128)}, u32[]{:S(2)}, u32[]{:S(2)}) collective-permute-start(f32[1536,1536]{1,0:T(8,128)} %broadcast_select_fusion), channel_id=1, source_target_pairs={{0,1},{1,0},{2,3},{3,2},{4,5},{5,4},{6,7},{7,6},{8,9},{9,8},{10,11... | collective-permute-start | bytes 28311560 | tf_op jit(solution)/shard_map/ppermute | solution.py:488
  517.4 15.3 %all-to-all-start.3 = ((f32[8,12,1280]{2,1,0:T(8,128)}), f32[8,12,1280]{2,1,0:T(8,128)S(1)}, u32[]{:S(2)}, u32[]{:S(2)}) async-start(f32[8,12,1280]{2,1,0:T(8,128)} %reshape.433), calls=%async_computation.5 | async-start | bytes 1310720 | tf_op jit(solution)/shard_map/all_to_all | solution.py:523
  521.8 237.2 %reduce-scatter.6.cloned.1.call-start = ((), (), s32[]{:S(2)}) async-start(), calls=%async_computation.10 | async-start | bytes 7077888 | tf_op jit(solution)/shard_map/reduce_scatter | solution.py:389
  745.5 1.8 collective-permute-start.9
  758.8 3.6 collective-permute-start.10
  (188 other events, 1992.7 us)
Sparse Core Ops, SparseCore 0:
  9.7 32.5 all-gather.9
  45.0 54.4 all-gather.11
  101.2 27.8 all-gather.13
  213.3 73.5 reduce-scatter.9
  290.0 89.0 all-gather.17
  391.4 85.0 all-gather.15
  478.8 41.4 reduce-scatter.7
  527.7 42.8 reduce-scatter.5
